TPU v7x, 256 devices: a whole 4x4x8 slice. The times are simulated.
256 devices in a mesh: gx: 8 (over z), gy: 32 (over x, y, core).
Axes of the slice: x: 4, y: 4, z: 8, core: 2. Of those that a mesh axis runs over, the one named last changes fastest.
Arguments:
- rhs: float32 [4, 128, 131072], P(None, None, ('gx', 'gy')), may hold values from -6 to 6
- offsets: float32 [3, 128, 131072], P(None, None, ('gx', 'gy')), may hold values from -4 to 4
- lengths: float32 [131072], P(('gx', 'gy')), may hold values from 1 to 4
- bucket: int32 [131072, 1], P(('gx', 'gy')), may hold values from 0 to 7; in each aligned block of 512 rows (0 to 511, 512 to 1023, ...) at most 128 rows name the same one
- attach: int32 [131072], P(('gx', 'gy')), may hold values from 0 to 2047
- operator: float32 [8, 512, 512], P('gx'), may hold values from -0.25 to 0.25
- inverse: float32 [8, 512, 512], P('gx'), as said below
- mobility: float32 [36, 16384], P(None, ('gx', 'gy')), may hold values from -2.5 to 2.5
Outputs:
- velocity: float32 [4, 128, 131072], P(None, None, ('gx', 'gy'))
Inputs may be any that keep to these rules, and one draw needn't show every extreme that they name: Bucket b owns fibers of 16 * 2^(b mod 4) nodes. Among the 512 fibers of one device no bucket has more than 128, and in every draw some bucket has exactly 128 there. `inverse`: identity plus a dense full-rank part.
All inputs are finite; a program needn't handle non-finite values.
Results may differ from a plain program's by a relative error of at most 0.0003.
Values sent between devices are 32-bit elements; how exact they have to be, the bound alone decides.
A program may use at most 64 MiB of HBM per device.

v0:
```python
import jax
import jax.numpy as jnp
from jax import lax
from jax.experimental import pallas as pl
from jax.experimental.pallas import tpu as pltpu
from jax.sharding import PartitionSpec as P

ITERS = 4
FIB = 512
CEN = 64
MESH = pl.DeviceIdType.MESH
F32, BF16 = jnp.float32, jnp.bfloat16
NODES = (16, 32, 64, 128)


def dot_nn(a, b):
    return lax.dot_general(a, b, (((1,), (0,)), ((), ())), preferred_element_type=F32)


def dot_nt(a, b):
    return lax.dot_general(a, b, (((1,), (1,)), ((), ())), preferred_element_type=F32)


def split2(x):
    hi = x.astype(BF16)
    return hi, (x - hi.astype(F32)).astype(BF16)


def stack3(x):
    hi = x.astype(BF16).astype(F32)
    rest = x - hi
    mid = rest.astype(BF16).astype(F32)
    return jnp.concatenate([hi, mid, rest - mid, jnp.zeros_like(x)], axis=0).astype(BF16)


def sum3(r):
    return r[0:8] + r[8:16] + r[16:24]


def product(matrix, x, pad=None):
    hi, lo = split2(x)
    right = jnp.concatenate([hi, lo], axis=1)
    if pad is not None:
        zeros = jnp.zeros_like(right)
        right = jnp.concatenate([right, zeros] if pad == 0 else [zeros, right], axis=0)
    r = dot_nn(matrix, right)
    m = r.shape[0] // 2
    return r[:m, :128] + (r[:m, 128:] + r[m:, :128])


def kernel(
    rhs_h, off_h, len_ref, bucket_ref, attach_ref, op_h, inv_h, mob_ref, out_ref,
    rhs, off, gs, gp, gk, st, m3, m2, m1, m0, mt, xhl, onehot,
    src3, src2, src1, src0, geo3, geo2, geo1, geo0, x3, x2, x1, x0, fac, wr,
    tab, got, mot, mob,
    in_sem, st_sem, own_sem, zs_sem, zp_sem, zk_sem, zrs_sem, zrp_sem, zrk_sem,
    ring_s, ring_r, t_s, t_r, mo_s, mo_r, mob_s, mob_r,
):
    z = lax.axis_index("gx")
    g = lax.axis_index("gy")
    x, y, c = lax.div(g, 8), lax.rem(lax.div(g, 2), 4), lax.rem(g, 2)
    u, v = x + c * (y - x), y + c * (x - y)
    r = c * 16 + v * 4 + u
    level, bb = lax.rem(z, 4), lax.div(z, 4)

    def plane(vv, uu):
        xx, yy = uu + c * (vv - uu), vv + c * (uu - vv)
        return (z, (xx * 4 + yy) * 2 + c)

    u_up, u_down = lax.rem(u + 1, 4), lax.rem(u + 3, 4)
    v_up, v_down = lax.rem(v + 1, 4), lax.rem(v + 3, 4)
    sib = (z, g + 1 - 2 * c)

    def greet_line(d, n):
        pl.semaphore_signal(
            pltpu.get_barrier_semaphore(), inc=1, device_id=(lax.rem(z + d, 8), g), device_id_type=MESH
        )
        return n

    def greet_plane(d, n):
        pl.semaphore_signal(
            pltpu.get_barrier_semaphore(), inc=1, device_id=(z, lax.rem(g + d, 32)), device_id_type=MESH
        )
        return n

    lax.fori_loop(1, 8, greet_line, 0)
    lax.fori_loop(1, 32, greet_plane, 0)

    load_rhs = pltpu.make_async_copy(rhs_h, rhs, in_sem.at[0])
    load_off = pltpu.make_async_copy(off_h, off, in_sem.at[1])
    load_rhs.start()
    load_off.start()

    lane = lax.broadcasted_iota(jnp.int32, (8, 128), 1)

    def stage(row):
        row = pl.multiple_of(row, 8)
        a = pltpu.make_async_copy(inv_h.at[0, pl.ds(row, 8)], st.at[0], st_sem.at[0])
        b = pltpu.make_async_copy(op_h.at[0, pl.ds(row, 8)], st.at[1], st_sem.at[1])
        a.start()
        b.start()
        a.wait()
        b.wait()

    row3 = pl.multiple_of(r * 16, 16)

    @pl.when(level == 2)
    def _():
        stage(lax.div(r, 8) * 128 + lax.rem(r, 8) * 8)
        for m in range(2):
            for h in range(2):
                left = st[m, :, 256 * h : 256 * h + 128]
                right = st[m, :, 256 * h + 128 : 256 * h + 256]
                gs[c, v, u, bb, 2 + 2 * m + h] = jnp.where(lane < 64, left, pltpu.roll(right, 64, 1))

    @pl.when(level == 1)
    def _():
        q = lax.rem(r, 16)
        stage(lax.div(q, 4) * 128 + lax.rem(q, 4) * 8)
        total = jnp.zeros((8, 128), F32)
        for cc in range(4):
            part = jnp.where(c == 0, st[0, :, 128 * cc : 128 * cc + 128], st[1, :, 128 * cc : 128 * cc + 128])
            part = pltpu.roll(part, 32 * cc, 1) if cc else part
            total = jnp.where((lane >= 32 * cc) & (lane < 32 * cc + 32), part, total)
        gs[c, v, u, bb, 1] = total

    @pl.when(level == 0)
    def _():
        q = lax.rem(r, 8)
        stage(lax.div(q, 2) * 128 + lax.rem(q, 2) * 8)
        total = jnp.zeros((8, 128), F32)
        for m in range(2):
            for cc in range(4):
                at = 64 * m + 16 * cc
                part = st[m, :, 128 * cc : 128 * cc + 128]
                part = pltpu.roll(part, at, 1) if at else part
                total = jnp.where((lane >= at) & (lane < at + 16), part, total)
        gs[c, v, u, bb, 0] = total

    own_p = pltpu.make_async_copy(inv_h.at[0, pl.ds(row3, 16)], gp.at[c, v, u, bb], own_sem.at[0])
    own_k = pltpu.make_async_copy(op_h.at[0, pl.ds(row3, 16)], gk.at[c, v, u, bb], own_sem.at[1])

    @pl.when(level == 3)
    def _():
        own_p.start()
        own_k.start()

    pl.semaphore_wait(pltpu.get_barrier_semaphore(), 38)

    def line_copy(src, dst, sends, recv, d):
        return pltpu.make_async_remote_copy(
            src_ref=src, dst_ref=dst, send_sem=sends.at[d - 1], recv_sem=recv,
            device_id=(lax.rem(z + d, 8), g), device_id_type=MESH,
        )

    def small_slot(lev, b):
        first, count = ((0, 1), (1, 1), (2, 4))[lev]
        return gs.at[c, v, u, b, pl.ds(first, count)]

    def line_small(lev, b, d):
        slot = small_slot(lev, b)
        return line_copy(slot, slot, zs_sem, zrs_sem.at[lev, b], d)

    def line_p(b, d):
        return line_copy(inv_h.at[0, pl.ds(row3, 16)], gp.at[c, v, u, b], zp_sem, zrp_sem.at[b], d)

    def line_k(b, d):
        return line_copy(op_h.at[0, pl.ds(row3, 16)], gk.at[c, v, u, b], zk_sem, zrk_sem.at[b], d)

    for lev in range(3):

        @pl.when(level == lev)
        def _(lev=lev):
            for d in (4, 3, 5, 2, 6, 1, 7):
                line_small(lev, bb, d).start()

    @pl.when(level == 3)
    def _():
        for d in (4, 3, 5, 2, 6, 1, 7):
            line_p(bb, d).start()
        for d in (4, 3, 5, 2, 6, 1, 7):
            line_k(bb, d).start()

    def send(k, i, src, to):
        return pltpu.make_async_remote_copy(
            src_ref=src, dst_ref=src, send_sem=ring_s.at[k, i], recv_sem=ring_r.at[k, i],
            device_id=to, device_id_type=MESH,
        )

    def steps_of(k, b):
        v_far = lax.rem(v + 2, 4)
        return {
            "a": [send(k, 0, b.at[c, v, u], plane(v, u_up)), send(k, 1, b.at[c, v, u], plane(v, u_down))],
            "b": [send(k, 2, b.at[c, v, u_down, 0], plane(v, u_up)), send(k, 3, b.at[c, v, u_up, 1], plane(v, u_down))],
            "c": [send(k, 4, b.at[c, v], plane(v_up, u)), send(k, 5, b.at[c, v], plane(v_down, u))],
            "d": [
                send(k, 6, b.at[c, v_down, pl.ds(0, 2)], plane(v_up, u)),
                send(k, 7, b.at[c, v_up, pl.ds(2, 2)], plane(v_down, u)),
            ],
            "s0": [send(k, 8, b.at[c, v], sib)],
            "s1": [send(k, 9, b.at[c, v_down], sib), send(k, 10, b.at[c, v_up], sib)],
            "s2": [send(k, 11, b.at[c, v_far], sib)],
        }

    kinds = [steps_of(0, gs), steps_of(1, gp), steps_of(2, gk)]

    def go(k, *names):
        for name in names:
            for copy in kinds[k][name]:
                copy.start()

    def arrived(k, *names):
        for name in names:
            for copy in kinds[k][name]:
                copy.wait_recv()

    def from_line(k):
        if k == 0:
            for lev in range(3):
                for b in range(2):

                    @pl.when(z != 4 * b + lev)
                    def _(lev=lev, b=b):
                        line_small(lev, b, 1).wait_recv()

            return
        line, own = ((line_p, own_p), (line_k, own_k))[k - 1]
        for b in range(2):

            @pl.when(z != 4 * b + 3)
            def _(b=b):
                line(b, 1).wait_recv()

        @pl.when(level == 3)
        def _():
            own.wait()

    bucket = bucket_ref[...]
    own_level = jnp.bitwise_and(bucket, 3)
    counts = jnp.left_shift(jnp.full((1, FIB), 16, jnp.int32), own_level)
    marks = (lax.broadcasted_iota(jnp.int32, (16, FIB), 0) == bucket).astype(F32)
    before = lax.broadcasted_iota(jnp.int32, (FIB, FIB), 0) < lax.broadcasted_iota(jnp.int32, (FIB, FIB), 1)
    ranks = dot_nn(marks.astype(BF16), before.astype(F32).astype(BF16))
    rank = jnp.sum(ranks * marks, axis=0, keepdims=True)
    column = (own_level * 256 + jnp.right_shift(bucket, 2) * 128).astype(F32) + rank
    for i in range(8):
        place = (lax.broadcasted_iota(jnp.int32, (128, FIB), 0) + 128 * i).astype(F32)
        mt[128 * i : 128 * (i + 1), :] = (place == column).astype(F32).astype(BF16)

    load_rhs.wait()
    load_off.wait()
    for cc in range(7):
        hi, lo = split2(rhs[cc] if cc < 4 else off[cc - 4])
        xhl[256 * cc : 256 * cc + 128, :] = hi
        xhl[256 * cc + 128 : 256 * cc + 256, :] = lo

    srcs, geos, xs = (src0, src1, src2, src3), (geo0, geo1, geo2, geo3), (x0, x1, x2, x3)

    def regroup(lev):
        n = NODES[lev]
        slots = mt[256 * lev : 256 * lev + 256, :]
        if lev == 3:
            left = xhl[...]
        else:
            left = jnp.concatenate([xhl[128 * i : 128 * i + n, :] for i in range(14)], axis=0)
        moved = dot_nt(left, slots)
        for cc in range(7):
            value = moved[2 * n * cc : 2 * n * cc + n] + moved[2 * n * cc + n : 2 * n * cc + 2 * n]
            if cc < 4:
                srcs[lev][n * cc : n * cc + n, :] = value
            else:
                geos[lev][n * (cc - 4) : n * (cc - 4) + n, :] = value

    from_line(0)
    go(0, "a")

    coefficient = 0.3 / len_ref[...]
    hi = coefficient.astype(BF16).astype(F32)
    terms = jnp.where(lax.broadcasted_iota(jnp.int32, (16, FIB), 0) < 8, hi, coefficient - hi)
    factors = dot_nt(terms.astype(BF16), mt[...])
    fac[...] = factors[0:8] + factors[8:16]

    regroup(3)
    from_line(1)
    go(1, "a")
    arrived(0, "a")
    go(0, "b")
    regroup(2)
    from_line(2)
    go(2, "a")
    arrived(1, "a")
    go(1, "b")
    arrived(0, "b")
    go(0, "c", "s0")
    regroup(1)
    regroup(0)
    arrived(2, "a")
    go(2, "b")
    arrived(1, "b")
    go(1, "c", "s0")
    arrived(0, "c")
    go(0, "d", "s1")

    attach = attach_ref[...]

    def mark(i, n):
        start = pl.multiple_of(i * 256, 256)
        named = lax.broadcasted_iota(jnp.int32, (256, FIB), 0) + start
        onehot[pl.ds(start, 256), :] = (named == attach).astype(F32).astype(BF16)
        return n

    lax.fori_loop(0, 8, mark, 0)
    wide = jnp.concatenate([mob_ref[...], jnp.zeros((36, 64), F32)], axis=1)
    mob[c, 0:36, :] = jnp.where(c == 0, wide, pltpu.roll(wide, 64, 1))
    send_mob = pltpu.make_async_remote_copy(
        src_ref=mob.at[c], dst_ref=mob.at[c], send_sem=mob_s, recv_sem=mob_r, device_id=sib, device_id_type=MESH
    )
    send_mob.start()

    arrived(2, "b")
    go(2, "c", "s0")
    arrived(0, "d")
    go(0, "s2")

    def split_into(ref, i, matrix):
        hi, lo = split2(matrix)
        m = matrix.shape[0]
        ref[i, 0:m, :] = hi
        ref[i, m : 2 * m, :] = lo

    def sweep(lev, stiff, inverse):
        n = NODES[lev]
        held, geo, start = xs[lev], geos[lev], srcs[lev]
        for b in range(2):
            cols = slice(128 * b, 128 * b + 128)
            f = fac[0:1, 256 * lev + 128 * b : 256 * lev + 128 * b + 128]
            now = held[:, cols]
            pulled = stiff(b, now)
            o = [geo[n * i : n * i + n, cols] for i in range(3)]
            w = [now[n * i : n * i + n] for i in range(4)]
            along = 0.15 * (o[0] * w[0] + o[1] * w[1] + o[2] * w[2])
            across = along + 0.15 * w[3]
            held[:, cols] = start[:, cols] - f * pulled - jnp.concatenate(
                [o[0] * across, o[1] * across, o[2] * across, along], axis=0
            )
        for b in range(2):
            cols = slice(128 * b, 128 * b + 128)
            held[:, cols] = inverse(b, held[:, cols])

    arrived(0, "s0", "s1", "s2")
    for b in range(2):
        split_into(m0, b, gs[0, 0:2, :, b, 0].reshape(64, 128))
        split_into(m1, b, gs[0, :, :, b, 1].reshape(128, 128))
        split_into(m1, 2 + b, gs[1, :, :, b, 1].reshape(128, 128))
        for m in range(2):
            left, right = gs[:, :, :, b, 2 + 2 * m].reshape(256, 128), gs[:, :, :, b, 3 + 2 * m].reshape(256, 128)
            split_into(m2, 2 * m + b, jnp.concatenate([left, right], axis=1))

    inverses = (
        lambda b, w: product(m0[b], w, 0),
        lambda b, w: product(m1[b], w),
        lambda b, w: product(m2[b], w),
        lambda b, w: product(m3[b], w),
    )
    stiffs = (
        lambda b, w: product(m0[b], w, 1),
        lambda b, w: product(m1[2 + b], w),
        lambda b, w: product(m2[2 + b], w),
        lambda b, w: product(m3[2 + b], w),
    )

    def begin(lev):
        for b in range(2):
            cols = slice(128 * b, 128 * b + 128)
            xs[lev][:, cols] = inverses[lev](b, srcs[lev][:, cols])

    def small_sweeps(i, n):
        for lev in range(3):
            sweep(lev, stiffs[lev], inverses[lev])
        return n

    for lev in range(3):
        begin(lev)
    arrived(1, "c")
    go(1, "d", "s1")
    lax.fori_loop(0, 2, small_sweeps, 0)
    arrived(2, "c")
    go(2, "d", "s1")
    arrived(1, "d")
    go(1, "s2")
    lax.fori_loop(0, 2, small_sweeps, 0)

    arrived(1, "s0", "s1", "s2")
    for b in range(2):
        split_into(m3, b, gp[:, :, :, b].reshape(512, 512))
    begin(3)
    arrived(2, "d")
    go(2, "s2")
    arrived(2, "s0", "s1", "s2")
    for b in range(2):
        split_into(m3, 2 + b, gk[:, :, :, b].reshape(512, 512))

    def large_sweeps(i, n):
        sweep(3, stiffs[3], inverses[3])
        return n

    lax.fori_loop(0, ITERS, large_sweeps, 0)

    wr[...] = jnp.zeros_like(wr)
    for lev in range(4):
        n = NODES[lev]
        o = [geos[lev][n * i : n * i + n, :] for i in range(3)]
        w = [xs[lev][n * i : n * i + n, :] for i in range(3)]
        parts = w + [o[1] * w[2] - o[2] * w[1], o[2] * w[0] - o[0] * w[2], o[0] * w[1] - o[1] * w[0]]
        for i, part in enumerate(parts):
            wr[i : i + 1, 256 * lev : 256 * lev + 256] = jnp.sum(part, axis=0, keepdims=True)
    weight = len_ref[...] / counts.astype(F32)
    wrench = sum3(dot_nn(stack3(wr[...]), mt[...])) * weight
    table = sum3(dot_nt(stack3(wrench), onehot[...]))
    for q in range(16):
        tab[q] = table[:, 128 * q : 128 * q + 128]
    got[g] = tab[lax.div(g, 2)]

    def give(d):
        to = lax.rem(g + d, 32)
        return pltpu.make_async_remote_copy(
            src_ref=tab.at[lax.div(to, 2)], dst_ref=got.at[g], send_sem=t_s.at[d - 1], recv_sem=t_r.at[d - 1],
            device_id=(z, to), device_id_type=MESH,
        )

    def give_start(d, n):
        give(d).start()
        return n

    def give_wait(d, n):
        give(d).wait()
        return n

    lax.fori_loop(1, 32, give_start, 0)

    for lev in (3, 2, 1, 0):
        n = NODES[lev]
        hi, lo = split2(xs[lev][...])
        moved = dot_nn(jnp.concatenate([hi, lo], axis=0), mt[256 * lev : 256 * lev + 256, :])
        for cc in range(4):
            value = moved[n * cc : n * cc + n] + moved[4 * n + n * cc : 4 * n + n * cc + n]
            if lev == 3:
                out_ref[cc] = value
            else:
                out_ref[cc, 0:n, :] += value

    send_mob.wait()
    lax.fori_loop(1, 32, give_wait, 0)
    total = got[0]
    for i in range(1, 32):
        total = total + got[i]
    pair = mob[0, 0:36, :] + mob[1, 0:36, :]
    own_mot = lax.div(g, 2)
    rows = []
    for k in range(6):
        row = pair[6 * k : 6 * k + 1] * total[0:1]
        for j in range(1, 6):
            row = row + pair[6 * k + j : 6 * k + j + 1] * total[j : j + 1]
        rows.append(row)
    mot[own_mot] = jnp.concatenate(rows + [jnp.zeros((2, 128), F32)], axis=0)

    def tell(d):
        to = lax.rem(own_mot + d, 16)
        return pltpu.make_async_remote_copy(
            src_ref=mot.at[own_mot], dst_ref=mot.at[own_mot], send_sem=mo_s.at[d - 1], recv_sem=mo_r.at[d - 1],
            device_id=(z, to * 2 + c), device_id_type=MESH,
        )

    def tell_start(d, n):
        tell(d).start()
        return n

    def tell_wait(d, n):
        tell(d).wait()
        return n

    lax.fori_loop(1, 16, tell_start, 0)

    for steps in kinds:
        for copies in steps.values():
            for copy in copies:
                copy.wait_send()
    for lev in range(3):

        @pl.when(level == lev)
        def _(lev=lev):
            for d in range(1, 8):
                line_small(lev, bb, d).wait_send()

    @pl.when(level == 3)
    def _():
        for d in range(1, 8):
            line_p(bb, d).wait_send()
            line_k(bb, d).wait_send()

    lax.fori_loop(1, 16, tell_wait, 0)
    motions = jnp.concatenate([mot[q] for q in range(16)], axis=1)
    moving = sum3(dot_nn(stack3(motions), onehot[...]))
    live = lax.broadcasted_iota(jnp.int32, (128, FIB), 0) < counts
    o = [off[i] for i in range(3)]
    for i in range(3):
        j, k = (i + 1) % 3, (i + 2) % 3
        turn = moving[3 + j : 4 + j] * o[k] - moving[3 + k : 4 + k] * o[j]
        out_ref[i] += jnp.where(live, moving[i : i + 1] + turn, 0.0)


def body(rhs, offsets, lengths, bucket, attach, operator, inverse, mobility):
    any_ref, vmem = pl.BlockSpec(memory_space=pl.ANY), pl.BlockSpec(memory_space=pltpu.VMEM)
    dma = pltpu.SemaphoreType.DMA
    scratch = [
        pltpu.VMEM((4, 128, FIB), F32), pltpu.VMEM((3, 128, FIB), F32),
        pltpu.VMEM((2, 4, 4, 2, 6, 8, 128), F32),
        pltpu.VMEM((2, 4, 4, 2, 16, 512), F32), pltpu.VMEM((2, 4, 4, 2, 16, 512), F32),
        pltpu.VMEM((2, 8, 512), F32),
        pltpu.VMEM((4, 1024, 512), BF16), pltpu.VMEM((4, 512, 256), BF16),
        pltpu.VMEM((4, 256, 128), BF16), pltpu.VMEM((2, 128, 128), BF16),
        pltpu.VMEM((1024, FIB), BF16), pltpu.VMEM((7 * 256, FIB), BF16), pltpu.VMEM((32 * CEN, FIB), BF16),
        *[pltpu.VMEM((4 * n, 256), F32) for n in NODES[::-1]],
        *[pltpu.VMEM((3 * n, 256), F32) for n in NODES[::-1]],
        *[pltpu.VMEM((4 * n, 256), F32) for n in NODES[::-1]],
        pltpu.VMEM((8, 1024), F32), pltpu.VMEM((8, 1024), F32),
        pltpu.VMEM((16, 8, 128), F32), pltpu.VMEM((32, 8, 128), F32), pltpu.VMEM((16, 8, 128), F32),
        pltpu.VMEM((2, 40, 128), F32),
        dma((2,)), dma((2,)), dma((2,)), dma((7,)), dma((7,)), dma((7,)), dma((3, 2)), dma((2,)), dma((2,)),
        dma((3, 12)), dma((3, 12)), dma((31,)), dma((31,)), dma((15,)), dma((15,)), dma, dma,
    ]
    return pl.pallas_call(
        kernel,
        out_shape=jax.ShapeDtypeStruct((4, 128, FIB), F32),
        in_specs=[any_ref, any_ref, vmem, vmem, vmem, any_ref, any_ref, vmem],
        out_specs=vmem,
        scratch_shapes=scratch,
        compiler_params=pltpu.CompilerParams(
            collective_id=0, has_side_effects=True, vmem_limit_bytes=48 * 2**20
        ),
    )(
        rhs, offsets, lengths.reshape(1, FIB), bucket.reshape(1, FIB), attach.reshape(1, FIB),
        operator, inverse, mobility,
    )


def solution(mesh):
    both = ("gx", "gy")
    in_specs = (
        P(None, None, both), P(None, None, both), P(both), P(both, None), P(both),
        P("gx", None, None), P("gx", None, None), P(None, both),
    )
    return jax.shard_map(body, mesh=mesh, in_specs=in_specs, out_specs=P(None, None, both), check_vma=False)
```

profile of v0, /device:TPU:1, one launch (start us, length us, event | category | flops | bytes accessed | tf_op | source)
XLA Modules:
  0.0 69.4 jit_solution(13393105266410321921)
XLA Ops:
  0.0 0.0 copy-start.6
  0.0 0.0 copy-start.5
  0.0 0.7 copy-done.6
  0.7 0.0 copy-done.5
  0.7 0.0 copy-start
  0.7 1.2 %copy-done = f32[4,128,512]{2,1,0:T(8,128)S(1)} copy-done((f32[4,128,512]{2,1,0:T(8,128)S(1)}, f32[4,128,512]{2,1,0:T(8,128)}, u32[]{:S(2)}) %copy-start) | copy-done | bytes 1048600
  1.9 0.0 copy-start.1
  1.9 1.2 %copy-done.1 = f32[1,512,512]{2,1,0:T(8,128)S(1)} copy-done((f32[1,512,512]{2,1,0:T(8,128)S(1)}, f32[1,512,512]{2,1,0:T(8,128)}, u32[]{:S(2)}) %copy-start.1) | copy-done | bytes 1048600
  3.1 0.0 copy-start.2
  3.2 1.2 %copy-done.2 = f32[1,512,512]{2,1,0:T(8,128)S(1)} copy-done((f32[1,512,512]{2,1,0:T(8,128)S(1)}, f32[1,512,512]{2,1,0:T(8,128)}, u32[]{:S(2)}) %copy-start.2) | copy-done | bytes 1048600
  4.4 0.0 copy-start.3
  4.4 1.1 %copy-done.3 = f32[3,128,512]{2,1,0:T(8,128)S(1)} copy-done((f32[3,128,512]{2,1,0:T(8,128)S(1)}, f32[3,128,512]{2,1,0:T(8,128)}, u32[]{:S(2)}) %copy-start.3) | copy-done | bytes 786456
  5.5 0.0 copy-start.4
  5.5 0.7 %copy-done.4 = f32[36,64]{1,0:T(8,128)S(1)} copy-done((f32[36,64]{1,0:T(8,128)S(1)}, f32[36,64]{1,0:T(8,128)}, u32[]{:S(2)}) %copy-start.4) | copy-done | bytes 9240
  6.2 0.0 copy-start.7
  6.2 0.7 copy-done.7
  6.9 61.5 %shard_map.82 = f32[4,128,512]{2,1,0:T(8,128)S(1)} custom-call(f32[4,128,512]{2,1,0:T(8,128)S(1)} %copy-done, f32[3,128,512]{2,1,0:T(8,128)S(1)} %copy-done.3, f32[1,512]{1,0:T(1,128)S(1)} %bitcast.3, s32[1,512]{1,0:T(1,128)S(1)} %bitcast.4, s32[1,512]{1,0:T(1,128)S(1)} %bitcast.5, f32[1,512,512]{2,1,0:T(8,128)S(1)} %copy-done.1, ...), custom_call_target="tpu_custom_call" | custom-call | tf_op jit(solution)/shard_map/pallas_call | solution.py:532
  68.4 1.0 %copy.10 = f32[4,128,512]{2,1,0:T(8,128)} copy(f32[4,128,512]{2,1,0:T(8,128)S(1)} %shard_map.82) | data formatting | bytes 2097152
Async XLA Ops:
  0.0 0.7 copy-start.6
  0.0 0.7 %copy-start.5 = (f32[512]{0:T(512)S(1)}, f32[512]{0:T(512)}, u32[]{:S(2)}) copy-start(f32[512]{0:T(512)} %param.10) | copy-start | bytes 6148
  0.7 1.2 %copy-start = (f32[4,128,512]{2,1,0:T(8,128)S(1)}, f32[4,128,512]{2,1,0:T(8,128)}, u32[]{:S(2)}) copy-start(f32[4,128,512]{2,1,0:T(8,128)} %rhs_h.1) | copy-start | bytes 3145732
  1.9 1.2 %copy-start.1 = (f32[1,512,512]{2,1,0:T(8,128)S(1)}, f32[1,512,512]{2,1,0:T(8,128)}, u32[]{:S(2)}) copy-start(f32[1,512,512]{2,1,0:T(8,128)} %op_h.1) | copy-start | bytes 3145732
  3.1 1.2 %copy-start.2 = (f32[1,512,512]{2,1,0:T(8,128)S(1)}, f32[1,512,512]{2,1,0:T(8,128)}, u32[]{:S(2)}) copy-start(f32[1,512,512]{2,1,0:T(8,128)} %inv_h.1) | copy-start | bytes 3145732
  4.4 1.1 %copy-start.3 = (f32[3,128,512]{2,1,0:T(8,128)S(1)}, f32[3,128,512]{2,1,0:T(8,128)}, u32[]{:S(2)}) copy-start(f32[3,128,512]{2,1,0:T(8,128)} %off_h.1) | copy-start | bytes 2359300
  5.5 0.7 %copy-start.4 = (f32[36,64]{1,0:T(8,128)S(1)}, f32[36,64]{1,0:T(8,128)}, u32[]{:S(2)}) copy-start(f32[36,64]{1,0:T(8,128)} %mob_ref.1) | copy-start | bytes 27652
  6.2 0.7 copy-start.7
where the time goes:
time: 69.8 us; the launch traced here: 69.4 us
  Pallas kernels  61.5 us (88%)
  local copies, waits for them, and re-layouts  7.88 us (11%)
    pallas_call x1, Pallas kernels, body(): pl.pallas_call(kernel, out_shape=jax.ShapeDtypeStruct((4, 128, FIB), F32)...  61.5 us
    unnamed x17, local copies, waits for them, and re-layouts  7.88 us

commit v1 on v0

v1 whole, which is shorter than its diff:
```python
import jax
import jax.numpy as jnp
from jax import lax
from jax.experimental import pallas as pl
from jax.experimental.pallas import tpu as pltpu
from jax.sharding import PartitionSpec as P

ITERS = 4
FIB = 512
CEN = 64
MESH = pl.DeviceIdType.MESH
F32, BF16 = jnp.float32, jnp.bfloat16
NODES = (16, 32, 64, 128)


def dot_nn(a, b):
    return lax.dot_general(a, b, (((1,), (0,)), ((), ())), preferred_element_type=F32)


def dot_nt(a, b):
    return lax.dot_general(a, b, (((1,), (1,)), ((), ())), preferred_element_type=F32)


def split2(x):
    hi = x.astype(BF16)
    return hi, (x - hi.astype(F32)).astype(BF16)


def stack3(x):
    hi = x.astype(BF16).astype(F32)
    rest = x - hi
    mid = rest.astype(BF16).astype(F32)
    return jnp.concatenate([hi, mid, rest - mid, jnp.zeros_like(x)], axis=0).astype(BF16)


def sum3(r):
    return r[0:8] + r[8:16] + r[16:24]


def product(matrix, x):
    hi, lo = split2(x)
    m = matrix.shape[0] // 2
    first = dot_nn(matrix[...], hi)
    return first[:m] + (first[m:] + dot_nn(matrix[0:m, :], lo))


def kernel(
    rhs_h, off_h, len_h, bucket_h, attach_h, op_h, inv_h, mob_h, out_ref,
    len_ref, bucket_ref, attach_ref, mob_ref, rhs, off, gs, gp, gk, st, sg,
    m3, m2, m1, m0, mt, xhl, onehot, slothot,
    f3, f2, f1, f0, t3, t2, t1, t0, x3, x2, x1, x0, b3, b2, b1, b0, wr, asl,
    tab, got, mot, mob,
    in_sem, st_sem, own_sem, z_sem, zr_sem,
    ring_s, ring_r, fib_s, fib_r, back_s, back_r, t_s, t_r, mo_s, mo_r, mob_s, mob_r,
):
    z = lax.axis_index("gx")
    g = lax.axis_index("gy")
    x, y, c = lax.div(g, 8), lax.rem(lax.div(g, 2), 4), lax.rem(g, 2)
    u, v = x + c * (y - x), y + c * (x - y)
    level, bb = lax.rem(z, 4), lax.div(z, 4)
    ub, vb = x + bb * (y - x), y + bb * (x - y)
    rb = vb * 4 + ub
    away = c + bb - 2 * c * bb

    def plane(vv, uu):
        xx, yy = uu + c * (vv - uu), vv + c * (uu - vv)
        return (z, (xx * 4 + yy) * 2 + c)

    u_up, u_down = lax.rem(u + 1, 4), lax.rem(u + 3, 4)
    v_up, v_down = lax.rem(v + 1, 4), lax.rem(v + 3, 4)
    sib = (z, g + 1 - 2 * c)
    barrier = pltpu.get_barrier_semaphore()
    for d in range(1, 8):
        zz = lax.rem(z + d, 8)
        pl.semaphore_signal(barrier, inc=1, device_id=(zz, g), device_id_type=MESH)
        pl.semaphore_signal(barrier, inc=1, device_id=(zz, g + 1 - 2 * c), device_id_type=MESH)
    for d in range(1, 32):
        pl.semaphore_signal(barrier, inc=1, device_id=(z, lax.rem(g + d, 32)), device_id_type=MESH)

    load_rhs, load_off, load_bucket, load_len, load_attach, load_mob = loads = [
        pltpu.make_async_copy(source, place, in_sem.at[i])
        for i, (source, place) in enumerate((
            (rhs_h, rhs), (off_h, off), (bucket_h, bucket_ref),
            (len_h, len_ref), (attach_h, attach_ref), (mob_h, mob_ref),
        ))
    ]

    def stage(row, count):
        row = pl.multiple_of(row, 8)

        @pl.when(c == 0)
        def _():
            pltpu.make_async_copy(inv_h.at[0, pl.ds(row, count)], st.at[pl.ds(0, count)], st_sem).start()

        @pl.when(c == 1)
        def _():
            pltpu.make_async_copy(op_h.at[0, pl.ds(row, count)], st.at[pl.ds(0, count)], st_sem).start()

        for i in (2, 3, 4, 0, 1, 5):
            loads[i].start()
        pltpu.make_async_copy(inv_h.at[0, pl.ds(row, count)], st.at[pl.ds(0, count)], st_sem).wait()

    def lanes_of(rows):
        return lax.broadcasted_iota(jnp.int32, (rows, 128), 1)

    q1, q0 = rb, lax.rem(rb, 8)
    row3 = pl.multiple_of(rb * 32, 32)

    @pl.when(level == 2)
    def _():
        stage(lax.div(rb, 4) * 128 + lax.rem(rb, 4) * 16, 16)
        for h in range(2):
            left = st[:, 256 * h : 256 * h + 128]
            right = st[:, 256 * h + 128 : 256 * h + 256]
            part = jnp.where(lanes_of(16) < 64, left, pltpu.roll(right, 64, 1))
            sg[2 * h] = part[0:8]
            sg[2 * h + 1] = part[8:16]

    def compact(width):
        lane = lanes_of(8)
        total = jnp.zeros((8, 128), F32)
        for i in range(4):
            part = st[0:8, 128 * i : 128 * i + 128]
            part = pltpu.roll(part, width * i, 1) if i else part
            total = jnp.where((lane >= width * i) & (lane < width * i + width), part, total)
        sg[0] = total

    @pl.when(level == 1)
    def _():
        stage(lax.div(q1, 4) * 128 + lax.rem(q1, 4) * 8, 8)
        compact(32)

    @pl.when(level == 0)
    def _():
        stage(lax.div(q0, 2) * 128 + lax.rem(q0, 2) * 8, 8)
        compact(16)

    @pl.when(level == 3)
    def _():
        for i in (2, 3, 4, 0, 1, 5):
            loads[i].start()

    pl.semaphore_wait(barrier, 45)

    def rows_of(lev, m):
        if lev == 3:
            return (inv_h, op_h)[m].at[0, pl.ds(row3, 32)], (gp, gk)[m].at[vb, ub]
        first, count = ((m, 1), (2 + m, 1), (4 + 4 * m, 4))[lev]
        return sg.at[pl.ds(0, count)], gs.at[vb, ub, pl.ds(first, count)]

    def line(lev, m, d):
        source, slot = rows_of(lev, m)
        return pltpu.make_async_remote_copy(
            src_ref=source, dst_ref=slot, send_sem=z_sem.at[d], recv_sem=zr_sem.at[lev, m],
            device_id=(lax.rem(z + d, 8), g - c + bb), device_id_type=MESH,
        )

    def to_sibling(lev, m):
        source, slot = rows_of(lev, m)
        return pltpu.make_async_remote_copy(
            src_ref=source, dst_ref=slot, send_sem=z_sem.at[0], recv_sem=zr_sem.at[lev, m],
            device_id=sib, device_id_type=MESH,
        )

    def stays(lev, m):
        source, slot = rows_of(lev, m)
        return pltpu.make_async_copy(source, slot, own_sem.at[lev, m])

    for lev in range(4):
        for m in range(2):

            @pl.when((level == lev) & (c == m))
            def _(lev=lev, m=m):
                for d in (4, 3, 5, 2, 6, 1, 7):
                    line(lev, m, d).start()

            @pl.when((level == lev) & (c == m) & (bb != m))
            def _(lev=lev, m=m):
                to_sibling(lev, m).start()

            @pl.when((level == lev) & (c == m) & (bb == m))
            def _(lev=lev, m=m):
                stays(lev, m).start()

    def send(k, i, src, to):
        return pltpu.make_async_remote_copy(
            src_ref=src, dst_ref=src, send_sem=ring_s.at[k, i], recv_sem=ring_r.at[k, i],
            device_id=to, device_id_type=MESH,
        )

    def steps_of(k, b, half):
        return {
            "a": [send(k, 0, b.at[v, u], plane(v, u_up)), send(k, 1, b.at[v, u], plane(v, u_down))],
            "b": [
                send(k, 2, b.at[v, u_down, pl.ds(0, half)], plane(v, u_up)),
                send(k, 3, b.at[v, u_up, pl.ds(half, half)], plane(v, u_down)),
            ],
            "c": [send(k, 4, b.at[v], plane(v_up, u)), send(k, 5, b.at[v], plane(v_down, u))],
            "d": [
                send(k, 6, b.at[v_down, pl.ds(0, 2)], plane(v_up, u)),
                send(k, 7, b.at[v_up, pl.ds(2, 2)], plane(v_down, u)),
            ],
        }

    kinds = [steps_of(0, gs, 6), steps_of(1, gp, 16), steps_of(2, gk, 16)]

    def go(k, *names):
        for name in names:
            for copy in kinds[k][name]:
                copy.start()

    def arrived(k, *names):
        for name in names:
            for copy in kinds[k][name]:
                copy.wait_recv()

    def landing(lev, m):
        if lev == 3:
            slot = (gp, gk)[m].at[v, u]
        else:
            first, count = ((m, 1), (2 + m, 1), (4 + 4 * m, 4))[lev]
            slot = gs.at[v, u, pl.ds(first, count)]
        return pltpu.make_async_remote_copy(
            src_ref=slot, dst_ref=slot, send_sem=z_sem.at[0], recv_sem=zr_sem.at[lev, m],
            device_id=sib, device_id_type=MESH,
        )

    def from_line(k):
        for lev, m in (((0, 0), (0, 1), (1, 0), (1, 1), (2, 0), (2, 1)), ((3, 0),), ((3, 1),))[k]:

            @pl.when((z != 4 * c + lev) | (c != m))
            def _(lev=lev, m=m):
                landing(lev, m).wait_recv()

            @pl.when((z == 4 * c + lev) & (c == m))
            def _(lev=lev, m=m):
                stays(lev, m).wait()

    load_bucket.wait()
    load_len.wait()
    load_attach.wait()
    bucket = bucket_ref[...]
    own_level = jnp.bitwise_and(bucket, 3)
    counts = jnp.left_shift(jnp.full((1, FIB), 16, jnp.int32), own_level)
    marks = (lax.broadcasted_iota(jnp.int32, (16, FIB), 0) == bucket).astype(F32)
    before = lax.broadcasted_iota(jnp.int32, (FIB, FIB), 0) < lax.broadcasted_iota(jnp.int32, (FIB, FIB), 1)
    ranks = dot_nn(marks.astype(BF16), before.astype(F32).astype(BF16))
    rank = jnp.sum(ranks * marks, axis=0, keepdims=True)
    upper = jnp.right_shift(bucket, 2)
    other = upper + c - 2 * c * upper
    column = (own_level * 256 + other * 128).astype(F32) + rank
    for i in range(8):
        place = (lax.broadcasted_iota(jnp.int32, (128, FIB), 0) + 128 * i).astype(F32)
        mt[128 * i : 128 * (i + 1), :] = (place == column).astype(F32).astype(BF16)

    lengths = len_ref[...]
    attach = attach_ref[...]
    row = lax.broadcasted_iota(jnp.int32, (16, FIB), 0)
    which = jnp.bitwise_and(row, 7)
    extra = jnp.where(which == 0, 0.3 / lengths, jnp.where(which == 1, lengths / counts.astype(F32), 0.0))
    extra = jnp.where(which == 2, attach.astype(F32), extra)
    hi = extra.astype(BF16).astype(F32)
    xhl[1792:1808, :] = jnp.where(row < 8, hi, extra - hi).astype(BF16)

    load_rhs.wait()
    load_off.wait()
    for cc in range(7):
        hi, lo = split2(rhs[cc] if cc < 4 else off[cc - 4])
        xhl[256 * cc : 256 * cc + 128, :] = hi
        xhl[256 * cc + 128 : 256 * cc + 256, :] = lo

    fibers, leaving = (f0, f1, f2, f3), (t0, t1, t2, t3)
    xs, backs = (x0, x1, x2, x3), (b0, b1, b2, b3)

    def cross_over(lev):
        return pltpu.make_async_remote_copy(
            src_ref=leaving[lev], dst_ref=fibers[lev].at[c], send_sem=fib_s.at[lev], recv_sem=fib_r.at[lev],
            device_id=sib, device_id_type=MESH,
        )

    def come_back(lev):
        return pltpu.make_async_remote_copy(
            src_ref=xs[lev].at[1 - c], dst_ref=backs[lev], send_sem=back_s.at[lev], recv_sem=back_r.at[lev],
            device_id=sib, device_id_type=MESH,
        )

    def regroup(lev):
        n = NODES[lev]
        slots = mt[256 * lev : 256 * lev + 256, :]
        if lev == 3:
            left = xhl[...]
        else:
            left = jnp.concatenate([xhl[128 * i : 128 * i + n, :] for i in range(14)] + [xhl[1792:1808, :]], axis=0)
        moved = dot_nt(left, slots)
        for cc in range(7):
            value = moved[2 * n * cc : 2 * n * cc + n] + moved[2 * n * cc + n : 2 * n * cc + 2 * n]
            fibers[lev][c, n * cc : n * cc + n, :] = value[:, :128]
            leaving[lev][n * cc : n * cc + n, :] = value[:, 128:]
        value = moved[14 * n : 14 * n + 8] + moved[14 * n + 8 : 14 * n + 16]
        fibers[lev][c, 7 * n : 7 * n + 8, :] = value[:, :128]
        leaving[lev][7 * n : 7 * n + 8, :] = value[:, 128:]
        cross_over(lev).start()

    from_line(0)
    go(0, "a")
    for lev in (2, 1, 0):
        regroup(lev)
    arrived(0, "a")
    go(0, "b")
    from_line(1)
    go(1, "a")
    regroup(3)
    arrived(0, "b")
    go(0, "c")
    from_line(2)
    go(2, "a")
    arrived(1, "a")
    go(1, "b")

    def mark(i, n):
        start = pl.multiple_of(i * 256, 256)
        named = lax.broadcasted_iota(jnp.int32, (256, FIB), 0) + start
        onehot[pl.ds(start, 256), :] = (named == attach).astype(F32).astype(BF16)
        return n

    lax.fori_loop(0, 8, mark, 0)
    arrived(2, "a")
    go(2, "b")
    arrived(1, "b")
    go(1, "c")

    load_mob.wait()
    wide = jnp.concatenate([mob_ref[...], jnp.zeros((36, 64), F32)], axis=1)
    mob[c, 0:36, :] = jnp.where(c == 0, wide, pltpu.roll(wide, 64, 1))
    send_mob = pltpu.make_async_remote_copy(
        src_ref=mob.at[c], dst_ref=mob.at[c], send_sem=mob_s, recv_sem=mob_r, device_id=sib, device_id_type=MESH
    )
    send_mob.start()
    arrived(2, "b")
    go(2, "c")

    for lev in range(4):
        n = NODES[lev]
        cross_over(lev).wait_recv()
        for o in range(2):
            asl[0:1, 256 * lev + 128 * o : 256 * lev + 128 * o + 128] = fibers[lev][o, 7 * n + 2 : 7 * n + 3, :]
    arrived(0, "c")
    go(0, "d")
    named_by = asl[0:1, :]

    def mark_slots(i, n):
        start = pl.multiple_of(i * 128, 128)
        named = (lax.broadcasted_iota(jnp.int32, (128, 1024), 0) + start).astype(F32)
        slothot[pl.ds(start, 128), :] = (named == named_by).astype(F32).astype(BF16)
        return n

    lax.fori_loop(0, 16, mark_slots, 0)

    def split_into(ref, i, matrix):
        hi, lo = split2(matrix)
        m = matrix.shape[0]
        ref[i, 0:m, :] = hi
        ref[i, m : 2 * m, :] = lo

    mats = (m0, m1, m2, m3)

    def times(lev, i, w):
        if lev == 0:
            w = jnp.concatenate([w, jnp.zeros_like(w)], axis=0)
        return product(mats[lev].at[i], w)

    def both(ref, rows):
        return jnp.concatenate([ref[0, 0:rows, :], ref[1, 0:rows, :]], axis=1)

    def keep(lev, value):
        xs[lev][0] = value[:, :128]
        xs[lev][1] = value[:, 128:]

    def begin(lev):
        keep(lev, times(lev, 0, both(fibers[lev], 4 * NODES[lev])))

    def sweep(lev):
        n = NODES[lev]
        held, fib = xs[lev], fibers[lev]
        pulled = times(lev, 1, both(held, 4 * n))
        for o in range(2):
            f = fib[o, 7 * n : 7 * n + 1, :]
            a = [fib[o, n * (4 + i) : n * (5 + i), :] for i in range(3)]
            w = [held[o, n * i : n * i + n, :] for i in range(4)]
            along = 0.15 * (a[0] * w[0] + a[1] * w[1] + a[2] * w[2])
            across = along + 0.15 * w[3]
            for i in range(4):
                held[o, n * i : n * i + n, :] = (
                    fib[o, n * i : n * i + n, :]
                    - f * pulled[n * i : n * i + n, 128 * o : 128 * o + 128]
                    - (a[i] * across if i < 3 else along)
                )
        keep(lev, times(lev, 0, both(held, 4 * n)))

    def wrench_of(lev):
        n = NODES[lev]
        for o in range(2):
            a = [fibers[lev][o, n * (4 + i) : n * (5 + i), :] for i in range(3)]
            w = [xs[lev][o, n * i : n * i + n, :] for i in range(3)]
            weight = fibers[lev][o, 7 * n + 1 : 7 * n + 2, :]
            parts = w + [a[1] * w[2] - a[2] * w[1], a[2] * w[0] - a[0] * w[2], a[0] * w[1] - a[1] * w[0]]
            for i, part in enumerate(parts):
                wr[i : i + 1, 256 * lev + 128 * o : 256 * lev + 128 * o + 128] = (
                    jnp.sum(part, axis=0, keepdims=True) * weight
                )

    wr[...] = jnp.zeros_like(wr)
    arrived(0, "d")
    for m in range(2):
        split_into(m0, m, gs[0:2, :, m].reshape(64, 128))
        split_into(m1, m, gs[:, :, 2 + m].reshape(128, 128))
        left, right = [gs[:, :, 4 + 4 * m + 2 * h : 6 + 4 * m + 2 * h].reshape(256, 128) for h in range(2)]
        split_into(m2, m, jnp.concatenate([left, right], axis=1))
    for lev in range(3):
        begin(lev)
    arrived(1, "c")
    go(1, "d")

    def small_sweeps(i, n):
        for lev in range(3):
            sweep(lev)
        return n

    lax.fori_loop(0, 2, small_sweeps, 0)
    arrived(2, "c")
    go(2, "d")
    lax.fori_loop(0, 2, small_sweeps, 0)
    for lev in range(3):
        come_back(lev).start()
        wrench_of(lev)

    arrived(1, "d")
    split_into(m3, 0, gp[...].reshape(512, 512))
    begin(3)
    arrived(2, "d")
    split_into(m3, 1, gk[...].reshape(512, 512))

    def large_sweeps(i, n):
        sweep(3)
        return n

    lax.fori_loop(0, ITERS, large_sweeps, 0)
    come_back(3).start()
    wrench_of(3)
    table = sum3(dot_nt(stack3(wr[...]), slothot[...]))
    for q in range(16):
        tab[q] = table[:, 128 * q : 128 * q + 128]
    got[g] = tab[lax.div(g, 2)]
    for d in range(1, 32):
        to = lax.rem(g + d, 32)
        pltpu.make_async_remote_copy(
            src_ref=tab.at[lax.div(to, 2)], dst_ref=got.at[g], send_sem=t_s, recv_sem=t_r,
            device_id=(z, to), device_id_type=MESH,
        ).start()

    for lev in (2, 1, 0, 3):
        come_back(lev).wait_recv()
    for lev in (3, 2, 1, 0):
        n = NODES[lev]
        hi, lo = split2(jnp.concatenate([xs[lev][c], backs[lev][...]], axis=1))
        moved = dot_nn(jnp.concatenate([hi, lo], axis=0), mt[256 * lev : 256 * lev + 256, :])
        for cc in range(4):
            value = moved[n * cc : n * cc + n] + moved[4 * n + n * cc : 4 * n + n * cc + n]
            if lev == 3:
                out_ref[cc] = value
            else:
                out_ref[cc, 0:n, :] += value

    send_mob.wait()
    for lev in range(4):
        cross_over(lev).wait_send()
        come_back(lev).wait_send()
    for steps in kinds:
        for copies in steps.values():
            for copy in copies:
                copy.wait_send()
    for lev in range(4):
        for m in range(2):

            @pl.when((level == lev) & (c == m))
            def _(lev=lev, m=m):
                for d in range(1, 8):
                    line(lev, m, d).wait_send()

            @pl.when((level == lev) & (c == m) & (bb != m))
            def _(lev=lev, m=m):
                to_sibling(lev, m).wait_send()

    many = got.at[pl.ds(0, 31)]
    tables = pltpu.make_async_remote_copy(
        src_ref=many, dst_ref=many, send_sem=t_s, recv_sem=t_r, device_id=sib, device_id_type=MESH
    )
    tables.wait_send()
    tables.wait_recv()
    total = got[0]
    for i in range(1, 32):
        total = total + got[i]
    pair = mob[0, 0:36, :] + mob[1, 0:36, :]
    mine = lax.div(g, 2)
    rows = []
    for k in range(6):
        one = pair[6 * k : 6 * k + 1] * total[0:1]
        for j in range(1, 6):
            one = one + pair[6 * k + j : 6 * k + j + 1] * total[j : j + 1]
        rows.append(one)
    mot[mine] = jnp.concatenate(rows + [jnp.zeros((2, 128), F32)], axis=0)
    for d in range(1, 16):
        pltpu.make_async_remote_copy(
            src_ref=mot.at[mine], dst_ref=mot.at[mine], send_sem=mo_s, recv_sem=mo_r,
            device_id=(z, lax.rem(mine + d, 16) * 2 + c), device_id_type=MESH,
        ).start()
    most = mot.at[pl.ds(0, 15)]
    motions_come = pltpu.make_async_remote_copy(
        src_ref=most, dst_ref=most, send_sem=mo_s, recv_sem=mo_r, device_id=sib, device_id_type=MESH
    )
    motions_come.wait_send()
    motions_come.wait_recv()
    motions = jnp.concatenate([mot[q] for q in range(16)], axis=1)
    moving = sum3(dot_nn(stack3(motions), onehot[...]))
    live = lax.broadcasted_iota(jnp.int32, (128, FIB), 0) < counts
    a = [off[i] for i in range(3)]
    for i in range(3):
        j, k = (i + 1) % 3, (i + 2) % 3
        turn = moving[3 + j : 4 + j] * a[k] - moving[3 + k : 4 + k] * a[j]
        out_ref[i] += jnp.where(live, moving[i : i + 1] + turn, 0.0)


def body(rhs, offsets, lengths, bucket, attach, operator, inverse, mobility):
    hbm, vmem = pl.BlockSpec(memory_space=pltpu.HBM), pl.BlockSpec(memory_space=pltpu.VMEM)
    dma = pltpu.SemaphoreType.DMA
    scratch = [
        pltpu.VMEM((1, FIB), F32), pltpu.VMEM((1, FIB), jnp.int32), pltpu.VMEM((1, FIB), jnp.int32),
        pltpu.VMEM((36, CEN), F32),
        pltpu.VMEM((4, 128, FIB), F32), pltpu.VMEM((3, 128, FIB), F32),
        pltpu.VMEM((4, 4, 12, 8, 128), F32),
        pltpu.VMEM((4, 4, 32, 512), F32), pltpu.VMEM((4, 4, 32, 512), F32),
        pltpu.VMEM((16, 512), F32), pltpu.VMEM((4, 8, 128), F32),
        pltpu.VMEM((2, 1024, 512), BF16), pltpu.VMEM((2, 512, 256), BF16),
        pltpu.VMEM((2, 256, 128), BF16), pltpu.VMEM((2, 128, 128), BF16),
        pltpu.VMEM((1024, FIB), BF16), pltpu.VMEM((7 * 256 + 16, FIB), BF16), pltpu.VMEM((32 * CEN, FIB), BF16),
        pltpu.VMEM((32 * CEN, 1024), BF16),
        *[pltpu.VMEM((2, 7 * n + 8, 128), F32) for n in NODES[::-1]],
        *[pltpu.VMEM((7 * n + 8, 128), F32) for n in NODES[::-1]],
        *[pltpu.VMEM((2, 4 * n, 128), F32) for n in NODES[::-1]],
        *[pltpu.VMEM((4 * n, 128), F32) for n in NODES[::-1]],
        pltpu.VMEM((8, 1024), F32), pltpu.VMEM((8, 1024), F32),
        pltpu.VMEM((16, 8, 128), F32), pltpu.VMEM((32, 8, 128), F32), pltpu.VMEM((16, 8, 128), F32),
        pltpu.VMEM((2, 40, 128), F32),
        dma((6,)), dma, dma((4, 2)), dma((8,)), dma((4, 2)),
        dma((3, 8)), dma((3, 8)), dma((4,)), dma((4,)), dma((4,)), dma((4,)),
        dma, dma, dma, dma, dma, dma,
    ]
    return pl.pallas_call(
        kernel,
        out_shape=jax.ShapeDtypeStruct((4, 128, FIB), F32),
        in_specs=[hbm] * 8,
        out_specs=vmem,
        scratch_shapes=scratch,
        compiler_params=pltpu.CompilerParams(
            collective_id=0, has_side_effects=True, vmem_limit_bytes=60 * 2**20
        ),
    )(
        rhs, offsets, lengths.reshape(1, FIB), bucket.reshape(1, FIB), attach.reshape(1, FIB),
        operator, inverse, mobility,
    )


def solution(mesh):
    both = ("gx", "gy")
    in_specs = (
        P(None, None, both), P(None, None, both), P(both), P(both, None), P(both),
        P("gx", None, None), P("gx", None, None), P(None, both),
    )
    return jax.shard_map(body, mesh=mesh, in_specs=in_specs, out_specs=P(None, None, both), check_vma=False)
```

time: 69.8 us -> 70 us (level)
  Pallas kernels: 61.5 us -> 67.6 us
  local copies, waits for them, and re-layouts: 7.88 us -> 2.26 us
    pallas_call x1, Pallas kernels: 61.5 us -> 67.6 us  [body(): pl.pallas_call(kernel, out_shape=jax.ShapeDtypeStruct((4, 128, FIB), F32)...]
    unnamed x17 -> x1, local copies, waits for them, and re-layouts: 7.88 us -> 2.26 us
where the time goes in v1:
time: 70 us; the launch traced here: 69.9 us
  Pallas kernels  67.6 us (97%)
  local copies, waits for them, and re-layouts  2.26 us (3%)
    pallas_call x1, Pallas kernels, body(): pl.pallas_call(kernel, out_shape=jax.ShapeDtypeStruct((4, 128, FIB), F32)...  67.6 us
    unnamed x1, local copies, waits for them, and re-layouts  2.26 us

profile of v1, /device:TPU:1, one launch (start us, length us, event | category | flops | bytes accessed | tf_op | source)
XLA Modules:
  0.0 69.9 jit_solution(16783619682555264037)
XLA Ops:
  0.0 67.6 %shard_map.82 = f32[4,128,512]{2,1,0:T(8,128)} custom-call(f32[4,128,512]{2,1,0:T(8,128)} %rhs_h.1, f32[3,128,512]{2,1,0:T(8,128)} %off_h.1, f32[1,512]{1,0:T(1,128)} %bitcast.3, s32[1,512]{1,0:T(1,128)} %bitcast.4, s32[1,512]{1,0:T(1,128)} %bitcast.5, f32[1,512,512]{2,1,0:T(8,128)} %op_h.1, f32[1,512,512]{2,1,0:T(8,128)} %inv_h.1, f32[36,64]{1,0:T(8,128)} %mob_h.1), custom_call_target="tpu_custom_call" | custom-call | tf_op jit(solution)/shard_map/pallas_call | solution.py:558
  67.6 2.3 %copy.10 = f32[4,128,512]{2,1,0:T(8,128)} copy(f32[4,128,512]{2,1,0:T(8,128)} %shard_map.82) | data formatting | bytes 2097152

commit v2 on v1

--- a/solution.py
+++ b/solution.py
@@ -26,17 +26,6 @@
     return hi, (x - hi.astype(F32)).astype(BF16)
 
 
-def stack3(x):
-    hi = x.astype(BF16).astype(F32)
-    rest = x - hi
-    mid = rest.astype(BF16).astype(F32)
-    return jnp.concatenate([hi, mid, rest - mid, jnp.zeros_like(x)], axis=0).astype(BF16)
-
-
-def sum3(r):
-    return r[0:8] + r[8:16] + r[16:24]
-
-
 def product(matrix, x):
     hi, lo = split2(x)
     m = matrix.shape[0] // 2
@@ -45,12 +34,12 @@
 
 
 def kernel(
-    rhs_h, off_h, len_h, bucket_h, attach_h, op_h, inv_h, mob_h, out_ref,
-    len_ref, bucket_ref, attach_ref, mob_ref, rhs, off, gs, gp, gk, st, sg,
-    m3, m2, m1, m0, mt, xhl, onehot, slothot,
+    rhs_h, off_h, len_h, bucket_h, attach_h, op_h, inv_h, mob_h, sol_h, moving_ref,
+    len_ref, bucket_ref, attach_ref, mob_ref, rhs, off, gs, gp, gk, gpz, gkz, st, sg,
+    m3, m2, m1, m0, mt, xhl, fhot, shot, sol,
     f3, f2, f1, f0, t3, t2, t1, t0, x3, x2, x1, x0, b3, b2, b1, b0, wr, asl,
     tab, got, mot, mob,
-    in_sem, st_sem, own_sem, z_sem, zr_sem,
+    sol_sem, in_sem, st_sem, own_sem, z_sem, zz_sem, zr_sem,
     ring_s, ring_r, fib_s, fib_r, back_s, back_r, t_s, t_r, mo_s, mo_r, mob_s, mob_r,
 ):
     z = lax.axis_index("gx")
@@ -68,6 +57,7 @@
 
     u_up, u_down = lax.rem(u + 1, 4), lax.rem(u + 3, 4)
     v_up, v_down = lax.rem(v + 1, 4), lax.rem(v + 3, 4)
+    u_far = lax.rem(u + 2, 4)
     sib = (z, g + 1 - 2 * c)
     barrier = pltpu.get_barrier_semaphore()
     for d in range(1, 8):
@@ -104,7 +94,7 @@
         return lax.broadcasted_iota(jnp.int32, (rows, 128), 1)
 
     q1, q0 = rb, lax.rem(rb, 8)
-    row3 = pl.multiple_of(rb * 32, 32)
+    row3 = pl.multiple_of(rb * 24, 8)
 
     @pl.when(level == 2)
     def _():
@@ -143,22 +133,24 @@
     pl.semaphore_wait(barrier, 45)
 
     def rows_of(lev, m):
+        if lev == 4:
+            return (inv_h, op_h)[m].at[0, pl.ds(384, 128)], (gpz, gkz)[m]
         if lev == 3:
-            return (inv_h, op_h)[m].at[0, pl.ds(row3, 32)], (gp, gk)[m].at[vb, ub]
+            return (inv_h, op_h)[m].at[0, pl.ds(row3, 24)], (gp, gk)[m].at[vb, ub]
         first, count = ((m, 1), (2 + m, 1), (4 + 4 * m, 4))[lev]
         return sg.at[pl.ds(0, count)], gs.at[vb, ub, pl.ds(first, count)]
 
     def line(lev, m, d):
         source, slot = rows_of(lev, m)
         return pltpu.make_async_remote_copy(
-            src_ref=source, dst_ref=slot, send_sem=z_sem.at[d], recv_sem=zr_sem.at[lev, m],
+            src_ref=source, dst_ref=slot, send_sem=(zz_sem if lev == 4 else z_sem).at[d], recv_sem=zr_sem.at[lev, m],
             device_id=(lax.rem(z + d, 8), g - c + bb), device_id_type=MESH,
         )
 
     def to_sibling(lev, m):
         source, slot = rows_of(lev, m)
         return pltpu.make_async_remote_copy(
-            src_ref=source, dst_ref=slot, send_sem=z_sem.at[0], recv_sem=zr_sem.at[lev, m],
+            src_ref=source, dst_ref=slot, send_sem=(zz_sem if lev == 4 else z_sem).at[0], recv_sem=zr_sem.at[lev, m],
             device_id=sib, device_id_type=MESH,
         )
 
@@ -166,21 +158,24 @@
         source, slot = rows_of(lev, m)
         return pltpu.make_async_copy(source, slot, own_sem.at[lev, m])
 
-    for lev in range(4):
-        for m in range(2):
-
-            @pl.when((level == lev) & (c == m))
-            def _(lev=lev, m=m):
-                for d in (4, 3, 5, 2, 6, 1, 7):
-                    line(lev, m, d).start()
-
-            @pl.when((level == lev) & (c == m) & (bb != m))
-            def _(lev=lev, m=m):
-                to_sibling(lev, m).start()
-
-            @pl.when((level == lev) & (c == m) & (bb == m))
-            def _(lev=lev, m=m):
-                stays(lev, m).start()
+    def to_line(lev, m):
+        @pl.when((level == min(lev, 3)) & (c == m))
+        def _():
+            for d in (4, 3, 5, 2, 6, 1, 7):
+                line(lev, m, d).start()
+
+        @pl.when((level == min(lev, 3)) & (c == m) & (bb != m))
+        def _():
+            to_sibling(lev, m).start()
+
+        @pl.when((level == min(lev, 3)) & (c == m) & (bb == m))
+        def _():
+            stays(lev, m).start()
+
+    for lev in range(3):
+        to_line(lev, 0)
+        to_line(lev, 1)
+    to_line(3, 0)
 
     def send(k, i, src, to):
         return pltpu.make_async_remote_copy(
@@ -188,21 +183,17 @@
             device_id=to, device_id_type=MESH,
         )
 
-    def steps_of(k, b, half):
+    def steps_of(k, b):
         return {
-            "a": [send(k, 0, b.at[v, u], plane(v, u_up)), send(k, 1, b.at[v, u], plane(v, u_down))],
-            "b": [
-                send(k, 2, b.at[v, u_down, pl.ds(0, half)], plane(v, u_up)),
-                send(k, 3, b.at[v, u_up, pl.ds(half, half)], plane(v, u_down)),
-            ],
-            "c": [send(k, 4, b.at[v], plane(v_up, u)), send(k, 5, b.at[v], plane(v_down, u))],
+            "a": [send(k, i, b.at[v, u], plane(v, to)) for i, to in enumerate((u_up, u_down, u_far))],
+            "c": [send(k, 3, b.at[v], plane(v_up, u)), send(k, 4, b.at[v], plane(v_down, u))],
             "d": [
-                send(k, 6, b.at[v_down, pl.ds(0, 2)], plane(v_up, u)),
-                send(k, 7, b.at[v_up, pl.ds(2, 2)], plane(v_down, u)),
+                send(k, 5, b.at[v_down, pl.ds(0, 2)], plane(v_up, u)),
+                send(k, 6, b.at[v_up, pl.ds(2, 2)], plane(v_down, u)),
             ],
         }
 
-    kinds = [steps_of(0, gs, 6), steps_of(1, gp, 16), steps_of(2, gk, 16)]
+    kinds = [steps_of(0, gs), steps_of(1, gp), steps_of(2, gk)]
 
     def go(k, *names):
         for name in names:
@@ -215,7 +206,9 @@
                 copy.wait_recv()
 
     def landing(lev, m):
-        if lev == 3:
+        if lev == 4:
+            slot = (gpz, gkz)[m]
+        elif lev == 3:
             slot = (gp, gk)[m].at[v, u]
         else:
             first, count = ((m, 1), (2 + m, 1), (4 + 4 * m, 4))[lev]
@@ -226,13 +219,13 @@
         )
 
     def from_line(k):
-        for lev, m in (((0, 0), (0, 1), (1, 0), (1, 1), (2, 0), (2, 1)), ((3, 0),), ((3, 1),))[k]:
-
-            @pl.when((z != 4 * c + lev) | (c != m))
+        for lev, m in (((0, 0), (0, 1), (1, 0), (1, 1), (2, 0), (2, 1)), ((3, 0),), ((3, 1),), ((4, 0),), ((4, 1),))[k]:
+
+            @pl.when((z != 4 * c + min(lev, 3)) | (c != m))
             def _(lev=lev, m=m):
                 landing(lev, m).wait_recv()
 
-            @pl.when((z == 4 * c + lev) & (c == m))
+            @pl.when((z == 4 * c + min(lev, 3)) & (c == m))
             def _(lev=lev, m=m):
                 stays(lev, m).wait()
 
@@ -301,33 +294,25 @@
         leaving[lev][7 * n : 7 * n + 8, :] = value[:, 128:]
         cross_over(lev).start()
 
+    to_line(3, 1)
     from_line(0)
     go(0, "a")
-    for lev in (2, 1, 0):
-        regroup(lev)
-    arrived(0, "a")
-    go(0, "b")
     from_line(1)
     go(1, "a")
-    regroup(3)
-    arrived(0, "b")
+    to_line(4, 0)
+    regroup(2)
+    regroup(1)
+    regroup(0)
+    arrived(0, "a")
     go(0, "c")
     from_line(2)
     go(2, "a")
     arrived(1, "a")
-    go(1, "b")
-
-    def mark(i, n):
-        start = pl.multiple_of(i * 256, 256)
-        named = lax.broadcasted_iota(jnp.int32, (256, FIB), 0) + start
-        onehot[pl.ds(start, 256), :] = (named == attach).astype(F32).astype(BF16)
-        return n
-
-    lax.fori_loop(0, 8, mark, 0)
+    go(1, "c")
+    to_line(4, 1)
+    regroup(3)
     arrived(2, "a")
-    go(2, "b")
-    arrived(1, "b")
-    go(1, "c")
+    go(2, "c")
 
     load_mob.wait()
     wide = jnp.concatenate([mob_ref[...], jnp.zeros((36, 64), F32)], axis=1)
@@ -336,25 +321,23 @@
         src_ref=mob.at[c], dst_ref=mob.at[c], send_sem=mob_s, recv_sem=mob_r, device_id=sib, device_id_type=MESH
     )
     send_mob.start()
-    arrived(2, "b")
-    go(2, "c")
-
+    arrived(0, "c")
+    go(0, "d")
+
+    chip = jnp.right_shift(attach, 7)
+    place = lax.broadcasted_iota(jnp.int32, (128, FIB), 0)
+    fhot[...] = (place == jnp.bitwise_and(attach, 127)).astype(F32).astype(BF16)
     for lev in range(4):
         n = NODES[lev]
         cross_over(lev).wait_recv()
         for o in range(2):
             asl[0:1, 256 * lev + 128 * o : 256 * lev + 128 * o + 128] = fibers[lev][o, 7 * n + 2 : 7 * n + 3, :]
-    arrived(0, "c")
-    go(0, "d")
-    named_by = asl[0:1, :]
-
-    def mark_slots(i, n):
-        start = pl.multiple_of(i * 128, 128)
-        named = (lax.broadcasted_iota(jnp.int32, (128, 1024), 0) + start).astype(F32)
-        slothot[pl.ds(start, 128), :] = (named == named_by).astype(F32).astype(BF16)
-        return n
-
-    lax.fori_loop(0, 16, mark_slots, 0)
+    slot_chip = jnp.floor(asl[0:1, :] * (1 / 128))
+    slot_place = asl[0:1, :] - 128 * slot_chip
+    place = lax.broadcasted_iota(jnp.int32, (128, 1024), 0).astype(F32)
+    shot[...] = (place == slot_place).astype(F32).astype(BF16)
+    arrived(1, "c")
+    go(1, "d")
 
     def split_into(ref, i, matrix):
         hi, lo = split2(matrix)
@@ -379,23 +362,31 @@
     def begin(lev):
         keep(lev, times(lev, 0, both(fibers[lev], 4 * NODES[lev])))
 
+    def paired(lev, i, w):
+        hi, lo = split2(w)
+        right = jnp.concatenate([hi, lo], axis=1)
+        if lev == 0:
+            right = jnp.concatenate([right, jnp.zeros_like(right)], axis=0)
+        r = dot_nn(mats[lev][i], right)
+        m = r.shape[0] // 2
+        return r[:m, :128] + (r[:m, 128:] + r[m:, :128])
+
     def sweep(lev):
         n = NODES[lev]
         held, fib = xs[lev], fibers[lev]
-        pulled = times(lev, 1, both(held, 4 * n))
         for o in range(2):
+            now = held[o]
+            pulled = paired(lev, 1, now)
             f = fib[o, 7 * n : 7 * n + 1, :]
             a = [fib[o, n * (4 + i) : n * (5 + i), :] for i in range(3)]
-            w = [held[o, n * i : n * i + n, :] for i in range(4)]
+            w = [now[n * i : n * i + n, :] for i in range(4)]
             along = 0.15 * (a[0] * w[0] + a[1] * w[1] + a[2] * w[2])
             across = along + 0.15 * w[3]
-            for i in range(4):
-                held[o, n * i : n * i + n, :] = (
-                    fib[o, n * i : n * i + n, :]
-                    - f * pulled[n * i : n * i + n, 128 * o : 128 * o + 128]
-                    - (a[i] * across if i < 3 else along)
-                )
-        keep(lev, times(lev, 0, both(held, 4 * n)))
+            left = [
+                fib[o, n * i : n * i + n, :] - f * pulled[n * i : n * i + n] - (a[i] * across if i < 3 else along)
+                for i in range(4)
+            ]
+            held[o] = paired(lev, 0, jnp.concatenate(left, axis=0))
 
     def wrench_of(lev):
         n = NODES[lev]
@@ -418,38 +409,42 @@
         split_into(m2, m, jnp.concatenate([left, right], axis=1))
     for lev in range(3):
         begin(lev)
-    arrived(1, "c")
-    go(1, "d")
 
     def small_sweeps(i, n):
         for lev in range(3):
             sweep(lev)
         return n
 
-    lax.fori_loop(0, 2, small_sweeps, 0)
+    lax.fori_loop(0, 1, small_sweeps, 0)
     arrived(2, "c")
     go(2, "d")
-    lax.fori_loop(0, 2, small_sweeps, 0)
+    lax.fori_loop(1, ITERS, small_sweeps, 0)
     for lev in range(3):
         come_back(lev).start()
         wrench_of(lev)
 
     arrived(1, "d")
-    split_into(m3, 0, gp[...].reshape(512, 512))
+    from_line(3)
+    split_into(m3, 0, jnp.concatenate([gp[...].reshape(384, 512), gpz[...]], axis=0))
     begin(3)
     arrived(2, "d")
-    split_into(m3, 1, gk[...].reshape(512, 512))
+    from_line(4)
+    split_into(m3, 1, jnp.concatenate([gk[...].reshape(384, 512), gkz[...]], axis=0))
 
     def large_sweeps(i, n):
         sweep(3)
         return n
 
-    lax.fori_loop(0, ITERS, large_sweeps, 0)
+    for i in range(ITERS):
+        large_sweeps(i, 0)
     come_back(3).start()
     wrench_of(3)
-    table = sum3(dot_nt(stack3(wr[...]), slothot[...]))
+    hi = wr[...].astype(BF16).astype(F32)
+    terms = jnp.concatenate([hi, wr[...] - hi], axis=0)
+    left = jnp.concatenate([jnp.where(slot_chip == q, terms, 0.0).astype(BF16) for q in range(16)], axis=0)
+    table = dot_nt(left, shot[...])
     for q in range(16):
-        tab[q] = table[:, 128 * q : 128 * q + 128]
+        tab[q] = table[16 * q : 16 * q + 8] + table[16 * q + 8 : 16 * q + 16]
     got[g] = tab[lax.div(g, 2)]
     for d in range(1, 32):
         to = lax.rem(g + d, 32)
@@ -467,9 +462,11 @@
         for cc in range(4):
             value = moved[n * cc : n * cc + n] + moved[4 * n + n * cc : 4 * n + n * cc + n]
             if lev == 3:
-                out_ref[cc] = value
+                sol[cc] = value
             else:
-                out_ref[cc, 0:n, :] += value
+                sol[cc, 0:n, :] += value
+    save = pltpu.make_async_copy(sol, sol_h, sol_sem)
+    save.start()
 
     send_mob.wait()
     for lev in range(4):
@@ -479,15 +476,15 @@
         for copies in steps.values():
             for copy in copies:
                 copy.wait_send()
-    for lev in range(4):
+    for lev in range(5):
         for m in range(2):
 
-            @pl.when((level == lev) & (c == m))
+            @pl.when((level == min(lev, 3)) & (c == m))
             def _(lev=lev, m=m):
                 for d in range(1, 8):
                     line(lev, m, d).wait_send()
 
-            @pl.when((level == lev) & (c == m) & (bb != m))
+            @pl.when((level == min(lev, 3)) & (c == m) & (bb != m))
             def _(lev=lev, m=m):
                 to_sibling(lev, m).wait_send()
 
@@ -520,14 +517,25 @@
     )
     motions_come.wait_send()
     motions_come.wait_recv()
-    motions = jnp.concatenate([mot[q] for q in range(16)], axis=1)
-    moving = sum3(dot_nn(stack3(motions), onehot[...]))
-    live = lax.broadcasted_iota(jnp.int32, (128, FIB), 0) < counts
-    a = [off[i] for i in range(3)]
+    hi, lo = split2(mot[...].reshape(128, 128))
+    parts = dot_nn(jnp.concatenate([hi, lo], axis=0), fhot[...])
+    moving = jnp.zeros((8, FIB), F32)
+    for q in range(16):
+        moving = jnp.where(chip == q, parts[8 * q : 8 * q + 8] + parts[128 + 8 * q : 136 + 8 * q], moving)
+    moving_ref[...] = moving
+    save.wait()
+
+
+def add_motion(sol_ref, off_ref, moving_ref, bucket_ref, out_ref):
+    counts = jnp.left_shift(jnp.full((1, FIB), 16, jnp.int32), jnp.bitwise_and(bucket_ref[...], 3))
+    live = lax.broadcasted_iota(jnp.int32, (64, FIB), 0) + 64 * pl.program_id(0) < counts
+    moving = moving_ref[...]
+    a = [off_ref[i] for i in range(3)]
     for i in range(3):
         j, k = (i + 1) % 3, (i + 2) % 3
         turn = moving[3 + j : 4 + j] * a[k] - moving[3 + k : 4 + k] * a[j]
-        out_ref[i] += jnp.where(live, moving[i : i + 1] + turn, 0.0)
+        out_ref[i] = sol_ref[i] + jnp.where(live, moving[i : i + 1] + turn, 0.0)
+    out_ref[3] = sol_ref[3]
 
 
 def body(rhs, offsets, lengths, bucket, attach, operator, inverse, mobility):
@@ -538,12 +546,13 @@
         pltpu.VMEM((36, CEN), F32),
         pltpu.VMEM((4, 128, FIB), F32), pltpu.VMEM((3, 128, FIB), F32),
         pltpu.VMEM((4, 4, 12, 8, 128), F32),
-        pltpu.VMEM((4, 4, 32, 512), F32), pltpu.VMEM((4, 4, 32, 512), F32),
+        pltpu.VMEM((4, 4, 24, 512), F32), pltpu.VMEM((4, 4, 24, 512), F32),
+        pltpu.VMEM((128, 512), F32), pltpu.VMEM((128, 512), F32),
         pltpu.VMEM((16, 512), F32), pltpu.VMEM((4, 8, 128), F32),
         pltpu.VMEM((2, 1024, 512), BF16), pltpu.VMEM((2, 512, 256), BF16),
         pltpu.VMEM((2, 256, 128), BF16), pltpu.VMEM((2, 128, 128), BF16),
-        pltpu.VMEM((1024, FIB), BF16), pltpu.VMEM((7 * 256 + 16, FIB), BF16), pltpu.VMEM((32 * CEN, FIB), BF16),
-        pltpu.VMEM((32 * CEN, 1024), BF16),
+        pltpu.VMEM((1024, FIB), BF16), pltpu.VMEM((7 * 256 + 16, FIB), BF16), pltpu.VMEM((128, FIB), BF16),
+        pltpu.VMEM((128, 1024), BF16), pltpu.VMEM((4, 128, FIB), F32),
         *[pltpu.VMEM((2, 7 * n + 8, 128), F32) for n in NODES[::-1]],
         *[pltpu.VMEM((7 * n + 8, 128), F32) for n in NODES[::-1]],
         *[pltpu.VMEM((2, 4 * n, 128), F32) for n in NODES[::-1]],
@@ -551,23 +560,37 @@
         pltpu.VMEM((8, 1024), F32), pltpu.VMEM((8, 1024), F32),
         pltpu.VMEM((16, 8, 128), F32), pltpu.VMEM((32, 8, 128), F32), pltpu.VMEM((16, 8, 128), F32),
         pltpu.VMEM((2, 40, 128), F32),
-        dma((6,)), dma, dma((4, 2)), dma((8,)), dma((4, 2)),
-        dma((3, 8)), dma((3, 8)), dma((4,)), dma((4,)), dma((4,)), dma((4,)),
+        dma, dma((6,)), dma, dma((5, 2)), dma((8,)), dma((8,)), dma((5, 2)),
+        dma((3, 7)), dma((3, 7)), dma((4,)), dma((4,)), dma((4,)), dma((4,)),
         dma, dma, dma, dma, dma, dma,
     ]
-    return pl.pallas_call(
+    bucket = bucket.reshape(1, FIB)
+    solved, moving = pl.pallas_call(
         kernel,
-        out_shape=jax.ShapeDtypeStruct((4, 128, FIB), F32),
+        out_shape=(jax.ShapeDtypeStruct((4, 128, FIB), F32), jax.ShapeDtypeStruct((8, FIB), F32)),
         in_specs=[hbm] * 8,
-        out_specs=vmem,
+        out_specs=(hbm, vmem),
         scratch_shapes=scratch,
         compiler_params=pltpu.CompilerParams(
             collective_id=0, has_side_effects=True, vmem_limit_bytes=60 * 2**20
         ),
     )(
-        rhs, offsets, lengths.reshape(1, FIB), bucket.reshape(1, FIB), attach.reshape(1, FIB),
-        operator, inverse, mobility,
+        rhs, offsets, lengths.reshape(1, FIB), bucket, attach.reshape(1, FIB), operator, inverse, mobility,
     )
+
+    def nodes(rows):
+        return pl.BlockSpec((rows, 64, FIB), lambda i: (0, i, 0))
+
+    return pl.pallas_call(
+        add_motion,
+        grid=(2,),
+        out_shape=jax.ShapeDtypeStruct((4, 128, FIB), F32),
+        in_specs=[
+            nodes(4), nodes(3), pl.BlockSpec((8, FIB), lambda i: (0, 0)), pl.BlockSpec((1, FIB), lambda i: (0, 0)),
+        ],
+        out_specs=nodes(4),
+        compiler_params=pltpu.CompilerParams(vmem_limit_bytes=60 * 2**20),
+    )(solved, offsets, moving, bucket)
 
 
 def solution(mesh):

time: 70 us -> 56.9 us (0.81)
  the two profiles are of different devices: /device:TPU:1 before, /device:TPU:64 now
where the time goes in v2:
time: 56.9 us; the launch traced here: 56.8 us
  Pallas kernels  56.8 us (100%)
    pallas_call x1, Pallas kernels, body(): pl.pallas_call(kernel, out_shape=(jax.ShapeDtypeStruct((4, 128, FIB), F32...  54.4 us
    pallas_call x1, Pallas kernels, body(): pl.pallas_call(add_motion, grid=(2,), out_shape=jax.ShapeDtypeStruct((4,...  2.39 us

profile of v2, /device:TPU:64, one launch (start us, length us, event | category | flops | bytes accessed | tf_op | source)
XLA Modules:
  0.0 56.8 jit_solution(13499231421595258395)
XLA Ops:
  0.0 54.4 %shard_map.82 = (f32[4,128,512]{2,1,0:T(8,128)}, f32[8,512]{1,0:T(8,128)}) custom-call(f32[4,128,512]{2,1,0:T(8,128)} %rhs_h.1, f32[3,128,512]{2,1,0:T(8,128)} %off_ref.1, f32[1,512]{1,0:T(1,128)} %bitcast.5, s32[1,512]{1,0:T(1,128)} %bitcast.3, s32[1,512]{1,0:T(1,128)} %bitcast.6, f32[1,512,512]{2,1,0:T(8,128)} %op_h.1, f32[1,512,512]{2,1,0:T(8,128)} %inv_h.1, ...), custom_call_target="tpu_custom_call" | custom-call | tf_op jit(solution)/shard_map/pallas_call | solution.py:568
  54.4 2.4 %shard_map.83 = f32[4,128,512]{2,1,0:T(8,128)} custom-call(f32[4,128,512]{2,1,0:T(8,128)} %get-tuple-element.7.sol_ref, f32[3,128,512]{2,1,0:T(8,128)} %off_ref.1, f32[8,512]{1,0:T(8,128)} %get-tuple-element.8.moving_ref, s32[1,512]{1,0:T(1,128)} %bitcast.4), custom_call_target="tpu_custom_call" | custom-call | tf_op jit(solution)/shard_map/pallas_call | solution.py:584

commit v3 on v2

--- a/solution.py
+++ b/solution.py
@@ -35,11 +35,11 @@
 
 def kernel(
     rhs_h, off_h, len_h, bucket_h, attach_h, op_h, inv_h, mob_h, sol_h, moving_ref,
-    len_ref, bucket_ref, attach_ref, mob_ref, rhs, off, gs, gp, gk, gpz, gkz, st, sg,
+    len_ref, bucket_ref, attach_ref, mob_ref, rhs, off, gs, gp, gk, gpz, gkz, st, sg, whole, prow, pkr, xz,
     m3, m2, m1, m0, mt, xhl, fhot, shot, sol,
     f3, f2, f1, f0, t3, t2, t1, t0, x3, x2, x1, x0, b3, b2, b1, b0, wr, asl,
     tab, got, mot, mob,
-    sol_sem, in_sem, st_sem, own_sem, z_sem, zz_sem, zr_sem,
+    sol_sem, in_sem, st_sem, pk_sem, own_sem, z_sem, zz_sem, zr_sem,
     ring_s, ring_r, fib_s, fib_r, back_s, back_r, t_s, t_r, mo_s, mo_r, mob_s, mob_r,
 ):
     z = lax.axis_index("gx")
@@ -125,18 +125,41 @@
         stage(lax.div(q0, 2) * 128 + lax.rem(q0, 2) * 8, 8)
         compact(16)
 
+    product_loads = [
+        pltpu.make_async_copy(source, place, pk_sem.at[i])
+        for i, (source, place) in enumerate((
+            (inv_h.at[0, pl.ds(row3, 32)], prow.at[pl.ds(0, 32)]),
+            (inv_h.at[0, pl.ds(384, 128)], prow.at[pl.ds(32, 128)]),
+            (op_h.at[0], whole),
+        ))
+    ]
+
     @pl.when(level == 3)
     def _():
         for i in (2, 3, 4, 0, 1, 5):
             loads[i].start()
 
+    @pl.when((level == 3) & (c == 1))
+    def _():
+        for copy in product_loads:
+            copy.start()
+
+    @pl.when((level == 3) & (c == 1))
+    def _():
+        for copy in product_loads:
+            copy.wait()
+        hi, lo = split2(prow[...])
+        over, under = split2(whole[...])
+        first = dot_nn(jnp.concatenate([hi, lo], axis=0), over)
+        pkr[...] = first[:160] + (first[160:] + dot_nn(hi, under))
+
     pl.semaphore_wait(barrier, 45)
 
     def rows_of(lev, m):
         if lev == 4:
-            return (inv_h, op_h)[m].at[0, pl.ds(384, 128)], (gpz, gkz)[m]
+            return (pkr.at[pl.ds(32, 128)] if m else inv_h.at[0, pl.ds(384, 128)]), (gpz, gkz)[m]
         if lev == 3:
-            return (inv_h, op_h)[m].at[0, pl.ds(row3, 24)], (gp, gk)[m].at[vb, ub]
+            return (pkr.at[pl.ds(0, 24)] if m else inv_h.at[0, pl.ds(row3, 24)]), (gp, gk)[m].at[vb, ub]
         first, count = ((m, 1), (2 + m, 1), (4 + 4 * m, 4))[lev]
         return sg.at[pl.ds(0, count)], gs.at[vb, ub, pl.ds(first, count)]
 
@@ -255,6 +278,7 @@
     hi = extra.astype(BF16).astype(F32)
     xhl[1792:1808, :] = jnp.where(row < 8, hi, extra - hi).astype(BF16)
 
+    to_line(3, 1)
     load_rhs.wait()
     load_off.wait()
     for cc in range(7):
@@ -294,7 +318,6 @@
         leaving[lev][7 * n : 7 * n + 8, :] = value[:, 128:]
         cross_over(lev).start()
 
-    to_line(3, 1)
     from_line(0)
     go(0, "a")
     from_line(1)
@@ -310,9 +333,9 @@
     arrived(1, "a")
     go(1, "c")
     to_line(4, 1)
-    regroup(3)
     arrived(2, "a")
     go(2, "c")
+    regroup(3)
 
     load_mob.wait()
     wide = jnp.concatenate([mob_ref[...], jnp.zeros((36, 64), F32)], axis=1)
@@ -348,6 +371,8 @@
     mats = (m0, m1, m2, m3)
 
     def times(lev, i, w):
+        if lev == 3:
+            return product(m3.at[:, pl.ds(512, 512)], w)
         if lev == 0:
             w = jnp.concatenate([w, jnp.zeros_like(w)], axis=0)
         return product(mats[lev].at[i], w)
@@ -388,6 +413,20 @@
             ]
             held[o] = paired(lev, 0, jnp.concatenate(left, axis=0))
 
+    def large_sweep():
+        n = NODES[3]
+        for o in range(2):
+            f = f3[o, 7 * n : 7 * n + 1, :]
+            a = [f3[o, n * (4 + i) : n * (5 + i), :] for i in range(3)]
+            w = [x3[o, n * i : n * i + n, :] for i in range(4)]
+            along = 0.15 * (a[0] * w[0] + a[1] * w[1] + a[2] * w[2])
+            across = along + 0.15 * w[3]
+            hi, lo = split2(
+                jnp.concatenate([f * w[i] for i in range(4)] + [a[i] * across for i in range(3)] + [along], axis=0)
+            )
+            r = dot_nn(m3[...], jnp.concatenate([hi, lo], axis=1))
+            x3[o] = xz[o] - (r[:512, :128] + (r[:512, 128:] + r[512:, :128]))
+
     def wrench_of(lev):
         n = NODES[lev]
         for o in range(2):
@@ -425,18 +464,18 @@
 
     arrived(1, "d")
     from_line(3)
-    split_into(m3, 0, jnp.concatenate([gp[...].reshape(384, 512), gpz[...]], axis=0))
+    hi, lo = split2(jnp.concatenate([gp[...].reshape(384, 512), gpz[...]], axis=0))
+    m3[0:512, 512:1024] = hi
+    m3[512:1024, 512:1024] = lo
     begin(3)
+    xz[...] = x3[...]
     arrived(2, "d")
     from_line(4)
-    split_into(m3, 1, jnp.concatenate([gk[...].reshape(384, 512), gkz[...]], axis=0))
-
-    def large_sweeps(i, n):
-        sweep(3)
-        return n
-
+    hi, lo = split2(jnp.concatenate([gk[...].reshape(384, 512), gkz[...]], axis=0))
+    m3[0:512, 0:512] = hi
+    m3[512:1024, 0:512] = lo
     for i in range(ITERS):
-        large_sweeps(i, 0)
+        large_sweep()
     come_back(3).start()
     wrench_of(3)
     hi = wr[...].astype(BF16).astype(F32)
@@ -549,7 +588,9 @@
         pltpu.VMEM((4, 4, 24, 512), F32), pltpu.VMEM((4, 4, 24, 512), F32),
         pltpu.VMEM((128, 512), F32), pltpu.VMEM((128, 512), F32),
         pltpu.VMEM((16, 512), F32), pltpu.VMEM((4, 8, 128), F32),
-        pltpu.VMEM((2, 1024, 512), BF16), pltpu.VMEM((2, 512, 256), BF16),
+        pltpu.VMEM((512, 512), F32), pltpu.VMEM((160, 512), F32), pltpu.VMEM((160, 512), F32),
+        pltpu.VMEM((2, 512, 128), F32),
+        pltpu.VMEM((1024, 1024), BF16), pltpu.VMEM((2, 512, 256), BF16),
         pltpu.VMEM((2, 256, 128), BF16), pltpu.VMEM((2, 128, 128), BF16),
         pltpu.VMEM((1024, FIB), BF16), pltpu.VMEM((7 * 256 + 16, FIB), BF16), pltpu.VMEM((128, FIB), BF16),
         pltpu.VMEM((128, 1024), BF16), pltpu.VMEM((4, 128, FIB), F32),
@@ -560,7 +601,7 @@
         pltpu.VMEM((8, 1024), F32), pltpu.VMEM((8, 1024), F32),
         pltpu.VMEM((16, 8, 128), F32), pltpu.VMEM((32, 8, 128), F32), pltpu.VMEM((16, 8, 128), F32),
         pltpu.VMEM((2, 40, 128), F32),
-        dma, dma((6,)), dma, dma((5, 2)), dma((8,)), dma((8,)), dma((5, 2)),
+        dma, dma((6,)), dma, dma((3,)), dma((5, 2)), dma((8,)), dma((8,)), dma((5, 2)),
         dma((3, 7)), dma((3, 7)), dma((4,)), dma((4,)), dma((4,)), dma((4,)),
         dma, dma, dma, dma, dma, dma,
     ]

time: 56.9 us -> 56.1 us (0.986)
  Pallas kernels: 56.8 us -> 56 us
    pallas_call x1, Pallas kernels: 54.4 us -> 53.6 us  [body(): pl.pallas_call(kernel, out_shape=(jax.ShapeDtypeStruct((4, 128, FIB), F32...]
where the time goes in v3:
time: 56.1 us; the launch traced here: 56 us
  Pallas kernels  56 us (100%)
    pallas_call x1, Pallas kernels, body(): pl.pallas_call(kernel, out_shape=(jax.ShapeDtypeStruct((4, 128, FIB), F32...  53.6 us
    pallas_call x1, Pallas kernels, body(): pl.pallas_call(add_motion, grid=(2,), out_shape=jax.ShapeDtypeStruct((4,...  2.39 us

profile of v3, /device:TPU:64, one launch (start us, length us, event | category | flops | bytes accessed | tf_op | source)
XLA Modules:
  0.0 56.0 jit_solution(10088330921850232750)
XLA Ops:
  0.0 53.6 %shard_map.82 = (f32[4,128,512]{2,1,0:T(8,128)}, f32[8,512]{1,0:T(8,128)}) custom-call(f32[4,128,512]{2,1,0:T(8,128)} %rhs_h.1, f32[3,128,512]{2,1,0:T(8,128)} %off_ref.1, f32[1,512]{1,0:T(1,128)} %bitcast.5, s32[1,512]{1,0:T(1,128)} %bitcast.3, s32[1,512]{1,0:T(1,128)} %bitcast.6, f32[1,512,512]{2,1,0:T(8,128)} %op_h.1, f32[1,512,512]{2,1,0:T(8,128)} %inv_h.1, ...), custom_call_target="tpu_custom_call" | custom-call | tf_op jit(solution)/shard_map/pallas_call | solution.py:609
  53.6 2.4 %shard_map.83 = f32[4,128,512]{2,1,0:T(8,128)} custom-call(f32[4,128,512]{2,1,0:T(8,128)} %get-tuple-element.7.sol_ref, f32[3,128,512]{2,1,0:T(8,128)} %off_ref.1, f32[8,512]{1,0:T(8,128)} %get-tuple-element.8.moving_ref, s32[1,512]{1,0:T(1,128)} %bitcast.4), custom_call_target="tpu_custom_call" | custom-call | tf_op jit(solution)/shard_map/pallas_call | solution.py:625
